TPU v7x, 256 devices: a whole 4x4x8 slice. The times are simulated.
256 devices in a mesh: tiles: 128 (over x, z, y), chan: 2 (over core).
Axes of the slice: x: 4, y: 4, z: 8, core: 2. Of those that a mesh axis runs over, the one named last changes fastest.
Arguments:
- features: bfloat16 [64, 16384, 256], P('chan', 'tiles'), may hold values from -6 to 6
- tile_valid: int32 [2048, 32], P('tiles'), may hold values 0 or 1
- parent_owner: int32 [16384], P('tiles'), may hold values from 0 to 127, as said below
- w_first: bfloat16 [9, 64, 64], P(None, 'chan'), may hold values from -0.25 to 0.25
- w_second: bfloat16 [9, 64, 64], P(None, 'chan'), may hold values from -0.25 to 0.25
- w_merge: bfloat16 [4, 64, 64], P(None, None, 'chan'), may hold values from -0.375 to 0.375
Outputs:
- enhanced: bfloat16 [64, 16384, 256], P('chan', 'tiles')
- parents: bfloat16 [64, 24576, 64], P('chan', 'tiles')
Inputs may be any that keep to these rules, and one draw needn't show every extreme that they name: `parent_owner`: within the 128 parents whose children lie on one index of tiles, no owner appears more than 2 times, and some owner appears exactly 2 times for some index. Half of the owners own 3 * 64 parents in all, the other half 128 / 2.
All inputs are finite; a program needn't handle non-finite values. No bound on the sum of `tile_valid` on one device may be relied on, other than what follows from the above.
Results may differ from a plain program's by a relative error of at most 0.0052.
Values may be sent and summed in bfloat16 or wider, within the bound.
A program may use at most 128 MiB of HBM per device.

v0:
```python
import functools

import jax
import jax.numpy as jnp
from jax import lax
from jax.experimental import pallas as pl
from jax.experimental.pallas import tpu as pltpu
from jax.sharding import PartitionSpec as P

MESH = pl.DeviceIdType.MESH
F32, BF16 = jnp.float32, jnp.bfloat16
NT = 128
ROWS = 128
COLS = 256
HALF = 64
CH = 64
HC = 32
PAR = 128
CAP = 192
EMPTY = 2.0**100


def dot(a, b):
    return jnp.dot(a, b, preferred_element_type=F32)


def shifted_sum(z, shift, col):
    left = jnp.where(col >= shift, pltpu.roll(z[0:128], shift, 1), 0.0)
    right = jnp.where(col < COLS - shift, pltpu.roll(z[256:384], COLS - shift, 1), 0.0)
    return z[128:256] + left + right


def main_kernel(
    feat, mask, owner, w1h, w2h, wmh, perm,
    enh_out, recv,
    x, h, e, w1, w2, wm, mext, t1, tiles, tall, sel, s32, send,
    loc, snd, rcv, esem, tsem, asem,
):
    t = lax.axis_index("tiles")
    c = lax.axis_index("chan")
    sib = 1 - c
    down = lax.rem(t + 1, NT)
    up = lax.rem(t + NT - 1, NT)

    bar = pltpu.get_barrier_semaphore()

    def greet(i, carry):
        pl.semaphore_signal(
            bar, inc=1, device_id={"tiles": lax.rem(t + i, NT), "chan": c}, device_id_type=MESH
        )
        return carry

    lax.fori_loop(1, NT, greet, 0)
    pl.semaphore_signal(bar, inc=1, device_id={"tiles": t, "chan": sib}, device_id_type=MESH)
    pl.semaphore_signal(bar, inc=1, device_id={"tiles": down, "chan": sib}, device_id_type=MESH)
    pl.semaphore_signal(bar, inc=1, device_id={"tiles": up, "chan": sib}, device_id_type=MESH)
    pl.semaphore_wait(bar, NT + 2)

    my_ch = pl.ds(pl.multiple_of(c * HC, HC), HC)
    local = [
        (feat.at[pl.ds(61 * c, 67)], x.at[pl.ds(3 - 3 * c, 67), my_ch]),
        (mask.at[pl.ds(7 * c, 9)], mext.at[pl.ds(1 - c, 9)]),
        (w1h, w1.at[:, my_ch]),
        (w2h, w2.at[:, my_ch]),
        (wmh, wm.at[:, my_ch]),
    ]
    local = [pltpu.make_async_copy(a, b, loc.at[i]) for i, (a, b) in enumerate(local)]

    def remote(src, dst, ssem, rsem, tile, core):
        return pltpu.make_async_remote_copy(
            src, dst, ssem, rsem, device_id={"tiles": tile, "chan": core}, device_id_type=MESH
        )

    far = [
        remote(w1h, w1.at[:, my_ch], snd.at[0], rcv.at[0], t, sib),
        remote(feat.at[pl.ds(61 * sib, 67)], x.at[pl.ds(3 * c, 67), my_ch], snd.at[1], rcv.at[1], t, sib),
        remote(w2h, w2.at[:, my_ch], snd.at[2], rcv.at[2], t, sib),
        remote(wmh, wm.at[:, my_ch], snd.at[3], rcv.at[3], t, sib),
        remote(
            mask.at[pl.ds(15 - 15 * c, 1)], mext.at[pl.ds(9 * c, 1)], snd.at[4], rcv.at[4],
            lax.rem(t + 1 - 2 * c + NT, NT), c,
        ),
    ]
    halo = [
        remote(feat.at[pl.ds(ROWS - 3, 3)], x.at[pl.ds(0, 3), my_ch], snd.at[5], rcv.at[5 + c], down, 0),
        remote(feat.at[pl.ds(0, 3)], x.at[pl.ds(67, 3), my_ch], snd.at[6], rcv.at[5 + c], up, 1),
    ]
    for copy in halo + far + local:
        copy.start()

    own_row = jnp.broadcast_to(owner[...], (PAR, PAR))
    own_col = jnp.transpose(own_row.astype(F32))
    row_id = lax.broadcasted_iota(jnp.int32, (PAR, PAR), 0)
    col_id = lax.broadcasted_iota(jnp.int32, (PAR, PAR), 1)
    before = jnp.where((own_col == own_row.astype(F32)) & (row_id < col_id), 1.0, 0.0)
    rank = jnp.sum(before, axis=0, keepdims=True)
    for k in range(2):
        hit = (row_id == own_row) & (jnp.broadcast_to(rank, (PAR, PAR)) == float(k))
        sel[pl.ds(k * PAR, PAR)] = jnp.where(hit, 1.0, 0.0).astype(BF16)

    for copy in far + halo:
        copy.wait_send()
    for copy in local:
        copy.wait()
    for copy in far:
        copy.wait_recv()
    edge = x.at[pl.ds(67 * c, 3), pl.ds(0, HC)]
    for k in range(2):
        pltpu.make_async_copy(edge, edge, rcv.at[5 + k]).wait()

    @pl.when((t == 0) & (c == 0))
    def _():
        x[pl.ds(0, 3)] = jnp.zeros((3, CH, COLS), BF16)
        mext[pl.ds(0, 1)] = jnp.zeros((1, 8, COLS), F32)

    @pl.when((t == NT - 1) & (c == 1))
    def _():
        x[pl.ds(67, 3)] = jnp.zeros((3, CH, COLS), BF16)
        mext[pl.ds(9, 1)] = jnp.zeros((1, 8, COLS), F32)

    col = lax.broadcasted_iota(jnp.int32, (128, COLS), 1)

    def conv_one(m, carry):
        z = dot(w1[...].reshape(384, 256), x[pl.ds(2 * m, 4)].reshape(256, COLS))
        out = shifted_sum(z, 1, col).reshape(16, 8, COLS) * mext[(m + 3) // 4][None]
        out = jnp.maximum(out, 0.0).reshape(2, CH, COLS).astype(BF16)
        h[0, m] = out[0]
        h[1, m] = out[1]
        return carry

    lax.fori_loop(0, 34, conv_one, 0)

    def conv_two(q, carry):
        for n2 in range(2):
            n = 2 * q + n2
            for p in range(2):
                z = dot(w2[...].reshape(384, 256), h[p, pl.ds(2 * n, 4)].reshape(256, COLS))
                out = shifted_sum(z, 2, col).reshape(2, CH, COLS)
                for i in range(2):
                    r = 4 * n + p + 2 * i
                    row = (out[i] + x[r + 3].astype(F32)).reshape(8, 8, COLS)
                    row = row * mext[1 + q][None]
                    e[r] = row.reshape(CH, COLS).astype(BF16)
            four = e[pl.ds(4 * n, 4)].reshape(256, COLS)
            turned = lax.dot_general(
                perm[...], four, (((1,), (1,)), ((), ())), preferred_element_type=F32
            ).astype(BF16)
            t1[q, :, pl.ds(n2 * 256, 256)] = turned[0:128]
            t1[q, :, pl.ds(512 + n2 * 256, 256)] = turned[128:256]
        return carry

    lax.fori_loop(0, 8, conv_two, 0)

    e_own = pltpu.make_async_copy(e.at[:, my_ch], enh_out.at[pl.ds(HALF * c, HALF)], loc.at[0])
    e_own.start()
    e_far = remote(
        e.at[:, pl.ds(pl.multiple_of(sib * HC, HC), HC)], enh_out.at[pl.ds(HALF * c, HALF)],
        esem.at[0], esem.at[1], t, sib,
    )
    e_far.start()

    for q in range(8):
        g, tp = q // 2, q % 2
        merged = dot(t1[q], wm[...].reshape(1024, 256)).astype(BF16)
        for v in range(8):
            for k in range(2):
                tiles[k, pl.ds(g * 16, 16), pl.ds((v * 2 + tp) * 128, 128)] = merged[
                    v * 16 : v * 16 + 16, k * 128 : k * 128 + 128
                ]

    mine = pl.ds(pl.multiple_of(c * HALF, HALF), HALF)
    t_own = pltpu.make_async_copy(tiles.at[c], tall.at[mine], loc.at[1])
    t_far = remote(tiles.at[sib], tall.at[mine], tsem.at[0], tsem.at[1], t, sib)
    t_far.start()
    t_own.start()
    t_own.wait()
    t_far.wait()

    filled = jnp.sum(sel[...].astype(F32), axis=1, keepdims=True)
    for v in range(8):
        out = dot(sel[...], tall[:, pl.ds(v * 256, 256)])
        if v == 0:
            out = jnp.where(jnp.broadcast_to(filled, (256, 256)) > 0.5, out, EMPTY)
        for k in range(2):
            for d2 in range(2):
                s32[d2, pl.ds(v * 2 + k, 128, stride=16), :] = out[
                    k * 128 : k * 128 + 128, d2 * 128 : d2 * 128 + 128
                ]

    def narrow(i, carry):
        for d2 in range(2):
            part = s32[d2, pl.ds(pl.multiple_of(128 * i, 128), 128)]
            send[pl.ds(8 * i, 8), :, pl.ds(d2 * 128, 128)] = part.astype(BF16).reshape(8, 16, 128)
        return carry

    lax.fori_loop(0, 16, narrow, 0)

    def deliver(i, carry):
        d = lax.rem(t + i, NT)
        remote(send.at[d], recv.at[t], asem.at[0], asem.at[1], d, c).start()
        return carry

    lax.fori_loop(1, NT, deliver, 0)
    own = pltpu.make_async_copy(send.at[t], recv.at[t], loc.at[2])
    own.start()
    own.wait()
    e_own.wait()
    e_far.wait()
    others = recv.at[pl.ds(0, NT - 1)]
    gone = send.at[pl.ds(0, NT - 1)]
    pltpu.make_async_copy(gone, gone, asem.at[0]).wait()
    pltpu.make_async_copy(others, others, asem.at[1]).wait()


def main_call(feat, mask, owner, w1h, w2h, wmh, perm):
    any_ = pl.BlockSpec(memory_space=pl.ANY)
    vmem = pl.BlockSpec(memory_space=pltpu.VMEM)
    return pl.pallas_call(
        main_kernel,
        out_shape=(
            jax.ShapeDtypeStruct((ROWS, HC, COLS), BF16),
            jax.ShapeDtypeStruct((NT, 16, 256), BF16),
        ),
        in_specs=[any_, any_, vmem, any_, any_, any_, vmem],
        out_specs=(any_, any_),
        scratch_shapes=[
            pltpu.VMEM((70, CH, COLS), BF16),
            pltpu.VMEM((2, 34, CH, COLS), BF16),
            pltpu.VMEM((HALF, CH, COLS), BF16),
            pltpu.VMEM((6, CH, 256), BF16),
            pltpu.VMEM((6, CH, 256), BF16),
            pltpu.VMEM((16, CH, 256), BF16),
            pltpu.VMEM((10, 8, COLS), F32),
            pltpu.VMEM((8, 128, 1024), BF16),
            pltpu.VMEM((2, HALF, 2048), BF16),
            pltpu.VMEM((PAR, 2048), BF16),
            pltpu.VMEM((256, PAR), BF16),
            pltpu.VMEM((2, 2048, 128), F32),
            pltpu.VMEM((NT, 16, 256), BF16),
            pltpu.SemaphoreType.DMA((5,)),
            pltpu.SemaphoreType.DMA((7,)),
            pltpu.SemaphoreType.DMA((7,)),
            pltpu.SemaphoreType.DMA((2,)),
            pltpu.SemaphoreType.DMA((2,)),
            pltpu.SemaphoreType.DMA((2,)),
        ],
        compiler_params=pltpu.CompilerParams(
            collective_id=0, has_side_effects=True, vmem_limit_bytes=40 << 20
        ),
        name="convs_and_exchange",
    )(feat, mask, owner, w1h, w2h, wmh, perm)


def place_kernel(recv, p1, p2, out, r32, o):
    def widen(i, carry):
        for d2 in range(2):
            part = recv[pl.ds(8 * i, 8), :, pl.ds(d2 * 128, 128)].reshape(128, 128)
            r32[d2, pl.ds(pl.multiple_of(128 * i, 128), 128)] = part.astype(F32)
        return carry

    lax.fori_loop(0, 16, widen, 0)
    here = [jnp.where(r32[0, pl.ds(k, 128, stride=16), :] < EMPTY, 1.0, 0.0) for k in range(2)]
    first = (lax.broadcasted_iota(jnp.int32, (8, NT), 1) == 0).astype(BF16)
    count = lax.dot_general(
        first, (here[0] + here[1]).astype(BF16), (((1,), (1,)), ((), ())),
        preferred_element_type=F32,
    )
    src = lax.broadcasted_iota(jnp.int32, (NT, NT), 0)
    dst = lax.broadcasted_iota(jnp.int32, (NT, NT), 1)
    start = dot(count.astype(BF16), jnp.where(src < dst, 1.0, 0.0).astype(BF16))
    slot = lax.broadcasted_iota(jnp.int32, (CAP, NT), 0).astype(F32)
    count = jnp.broadcast_to(count[0:1], (CAP, NT))
    start = jnp.broadcast_to(start[0:1], (CAP, NT))
    pick = jnp.concatenate(
        [
            jnp.where((slot == start + float(k)) & (count > float(k)), 1.0, 0.0)
            for k in range(2)
        ],
        axis=1,
    ).astype(BF16)

    for v in range(8):
        got = jnp.concatenate(
            [
                jnp.concatenate(
                    [r32[d2, pl.ds(v * 2 + k, 128, stride=16), :] for d2 in range(2)], axis=1
                )
                for k in range(2)
            ],
            axis=0,
        ).astype(BF16)
        placed = dot(pick, got).astype(BF16)
        o[v] = dot(placed, p1[...])
    lane = lax.broadcasted_iota(jnp.int32, (CAP, 128), 1) // 32
    for q in range(8):
        w, pos = q // 4, q % 4
        halves = []
        for hv in range(2):
            acc = jnp.zeros((CAP, 128), F32)
            for i in range(4):
                part = o[hv * 4 + i, :, pl.ds(w * 128, 128)]
                if i != pos:
                    part = pltpu.roll(part, (32 * (i - pos)) % 128, 1)
                acc = jnp.where(lane == i, part, acc)
            halves.append(acc)
        last = dot(jnp.concatenate(halves, axis=1).astype(BF16), p2[...]).astype(BF16)
        for i in range(4):
            out[q * 4 + i] = last[:, i * 64 : i * 64 + 64]


def place_call(recv, p1, p2):
    vmem = pl.BlockSpec(memory_space=pltpu.VMEM)
    return pl.pallas_call(
        place_kernel,
        out_shape=jax.ShapeDtypeStruct((HC, CAP, 64), BF16),
        in_specs=[vmem, vmem, vmem],
        out_specs=vmem,
        scratch_shapes=[pltpu.VMEM((2, 2048, 128), F32), pltpu.VMEM((8, CAP, 256), F32)],
        compiler_params=pltpu.CompilerParams(vmem_limit_bytes=40 << 20),
        name="place_parents",
    )(recv, p1, p2)


def one_hot(index, size):
    return (index[:, None] == jnp.arange(size, dtype=jnp.int32)[None, :]).astype(BF16)


def toeplitz(w):
    taps = w.reshape(3, 3, HC, CH).transpose(1, 2, 0, 3).reshape(3, HC, 3 * CH)
    return jnp.stack(
        [
            jnp.pad(taps, ((0, 0), (0, 0), (0, CH))),
            jnp.pad(taps, ((0, 0), (0, 0), (CH, 0))),
        ],
        axis=1,
    ).reshape(6, HC, 4 * CH)


def merge_weights(w):
    w = w.reshape(2, 2, 2, HC, HC).transpose(1, 0, 4, 2, 3)
    eye = jnp.eye(4, dtype=BF16)
    full = w[:, None, :, :, :, None, :] * eye[None, :, None, None, None, :, None]
    return full.reshape(16, HC, 256)


def on_device(features, tile_valid, parent_owner, w_first, w_second, w_merge):
    feat = jnp.transpose(features, (1, 0, 2))
    mask = jnp.broadcast_to(
        jnp.repeat(tile_valid.astype(F32), 8, axis=1)[:, None, :], (16, 8, COLS)
    )
    ids = jnp.arange(256, dtype=jnp.int32)
    b, v, j = ids // 128, ids // 16 % 8, ids % 16
    perm = one_hot(16 * j + 2 * v + b, 256)
    u, o = ids // 32, ids % 32
    p1 = one_hot(o // 4 * 32 + u * 4 + o % 4, 256)
    v2, u2, o2 = ids // 32, ids // 4 % 8, ids % 4
    p2 = one_hot(o2 * 64 + u2 * 8 + v2, 256)
    enh, recv = main_call(
        feat, mask, parent_owner.reshape(1, PAR), toeplitz(w_first), toeplitz(w_second),
        merge_weights(w_merge), perm,
    )
    parents = place_call(recv, p1, p2)
    return (jnp.transpose(enh, (1, 0, 2)), parents)


def solution(mesh):
    return jax.shard_map(
        on_device,
        mesh=mesh,
        in_specs=(
            P("chan", "tiles", None),
            P("tiles", None),
            P("tiles"),
            P(None, "chan", None),
            P(None, "chan", None),
            P(None, None, "chan"),
        ),
        out_specs=(P("chan", "tiles", None), P("chan", "tiles", None)),
        check_vma=False,
    )
```

profile of v0, /device:TPU:1, one launch (start us, length us, event | category | flops | bytes accessed | tf_op | source)
XLA Modules:
  0.0 84.2 jit_solution(11168053324156209121)
XLA Ops:
  0.6 0.9 %copy.30 = bf16[3,3,32,64]{3,0,2,1:T(4,128)(2,1)S(1)} copy(bf16[3,3,32,64]{3,2,1,0:T(8,128)(2,1)} %bitcast.36) | data formatting | bytes 73728 | tf_op jit(solution)/shard_map/reshape | solution.py:329
  1.6 0.1 reshape.171
  1.7 0.1 pad_bitcast_fusion.1
  1.8 0.9 %copy.31 = bf16[3,3,32,64]{3,0,2,1:T(4,128)(2,1)S(1)} copy(bf16[3,3,32,64]{3,2,1,0:T(8,128)(2,1)} %bitcast.37) | data formatting | bytes 73728 | tf_op jit(solution)/shard_map/reshape | solution.py:329
  2.8 0.1 reshape.168
  2.9 0.1 pad_bitcast_fusion.3
  3.0 0.0 copy-start.2
  3.0 2.8 %copy.29 = bf16[32,128,256]{2,0,1:T(8,128)(2,1)S(1)} copy(bf16[32,128,256]{2,1,0:T(8,128)(2,1)} %param.6) | data formatting | bytes 4194304 | tf_op args[0]
  5.8 0.0 copy-start.3
  5.8 0.0 copy-start.1
  5.8 0.0 copy-done.2
  5.8 0.1 reshape.173
  6.0 0.4 mul.72
  6.4 1.4 %mul.73 = bf16[16,32,256]{2,1,0:T(8,128)(2,1)} reshape(bf16[2,4,2,32,2,4,32]{6,5,4,3,2,1,0:T(4,128)(2,1)S(1)} %mul.72) | data formatting | bytes 524288 | tf_op jit(solution)/shard_map/mul | solution.py:342
  7.9 0.1 mul.74
  7.9 0.1 mul.75
  8.0 1.0 %broadcast_multiply_fusion.wmh = bf16[16,32,256]{2,1,0:T(8,128)(2,1)S(1)} fusion(bf16[16,32,256]{2,1,0:T(8,128)(2,1)} %mul.73, bf16[16,256]{1,0:T(8,128)(2,1)S(1)} %mul.75), kind=kLoop, calls=%fused_computation.7 | loop fusion | flops 131072 | bytes 532480 | tf_op jit(solution)/shard_map/mul | solution.py:342
  9.0 0.0 copy-done.3
  9.0 0.1 copy.17
  9.1 0.1 copy.18
  9.2 0.1 fusion.perm
  9.3 0.0 copy-done.1
  9.3 65.1 %convs_and_exchange.1 = (bf16[128,32,256]{2,1,0:T(8,128)(2,1)S(1)}, bf16[128,16,256]{2,1,0:T(8,128)(2,1)S(1)}) custom-call(bf16[128,32,256]{2,1,0:T(8,128)(2,1)S(1)} %bitcast.28, f32[16,8,256]{2,1,0:T(8,128)S(1)} %broadcast_in_dim.8.mask, s32[1,128]{1,0:T(1,128)S(1)} %bitcast.32, bf16[6,32,256]{2,1,0:T(8,128)(2,1)S(1)} %bitcast.31, ...), custom_call_target="tpu_custom_call" | custom-call | tf_op jit(solution)/shard_map/convs_and_exchange/pallas_call | solution.py:218
  74.5 0.0 copy-start
  74.5 1.3 %copy-done = bf16[128,32,256]{2,1,0:T(8,128)(2,1)} copy-done((bf16[128,32,256]{2,1,0:T(8,128)(2,1)}, bf16[128,32,256]{2,1,0:T(8,128)(2,1)S(1)}, u32[]{:S(2)}) %copy-start) | copy-done | bytes 2097176
  75.9 0.1 fusion.1
  76.0 2.5 %place_parents.1 = bf16[32,192,64]{2,1,0:T(8,128)(2,1)S(1)} custom-call(bf16[128,16,256]{2,1,0:T(8,128)(2,1)S(1)} %get-tuple-element.5.recv, bf16[256,256]{1,0:T(8,128)(2,1)S(1)} %get-tuple-element.14.p1, bf16[256,256]{1,0:T(8,128)(2,1)S(1)} %get-tuple-element.15.p2), custom_call_target="tpu_custom_call" | custom-call | tf_op jit(solution)/shard_map/place_parents/pallas_call | solution.py:313
  78.5 1.6 %copy.25 = bf16[32,192,64]{1,2,0:T(8,128)(2,1)} copy(bf16[32,192,64]{2,1,0:T(8,128)(2,1)S(1)} %place_parents.1) | data formatting | bytes 1572864
  80.1 4.1 %copy.24 = bf16[32,128,256]{2,1,0:T(8,128)(2,1)} copy(bf16[32,128,256]{2,0,1:T(8,128)(2,1)} %bitcast.29) | data formatting | bytes 4194304
  (12 shorter events, 0.2 us)
Async XLA Ops:
  3.0 2.8 %copy-start.2 = (bf16[4,64,32]{1,2,0:T(8,128)(2,1)S(1)}, bf16[4,64,32]{1,2,0:T(8,128)(2,1)}, u32[]{:S(2)}) copy-start(bf16[4,64,32]{1,2,0:T(8,128)(2,1)} %param.11) | copy-start | bytes 49156
  5.8 3.2 %copy-start.3 = (s32[16,32]{1,0:T(8,128)S(1)}, s32[16,32]{1,0:T(8,128)}, u32[]{:S(2)}) copy-start(s32[16,32]{1,0:T(8,128)} %param.7) | copy-start | bytes 6148
  5.8 3.5 %copy-start.1 = (s32[128]{0:T(128)S(1)}, s32[128]{0:T(128)}, u32[]{:S(2)}) copy-start(s32[128]{0:T(128)} %param.8) | copy-start | bytes 1540
  74.5 1.3 %copy-start = (bf16[128,32,256]{2,1,0:T(8,128)(2,1)}, bf16[128,32,256]{2,1,0:T(8,128)(2,1)S(1)}, u32[]{:S(2)}) copy-start(bf16[128,32,256]{2,1,0:T(8,128)(2,1)S(1)} %get-tuple-element.4) | copy-start | bytes 6291460
where the time goes:
time: 85.5 us; the launch traced here: 84.2 us
  Pallas kernels  67.7 us (79%)
  local copies, waits for them, and re-layouts  14.5 us (17%)
  other arithmetic  1.27 us (1%)
    pallas_call x1, Pallas kernels, main_call(): pl.pallas_call(main_kernel, out_shape=(jax.ShapeDtypeStruct((ROWS, HC, CO...  65.1 us
    unnamed x11, local copies, waits for them, and re-layouts  9.8 us
    pallas_call x1, Pallas kernels, place_call(): pl.pallas_call(place_kernel, out_shape=jax.ShapeDtypeStruct((HC, CAP, 64)...  2.55 us
    reshape x4, local copies, waits for them, and re-layouts, toeplitz(): taps = w.reshape(3, 3, HC, CH).transpose(1, 2, 0, 3).reshape(3, HC, 3 * CH)  2.12 us
    mul x4, local copies, waits for them, and re-layouts, merge_weights(): w[:, None, :, :, :, None, :] * eye[None, :, None, None, None, :, None]  2.05 us

commit v1 on v0

v1 whole, which is shorter than its diff:
```python
import functools

import jax
import jax.numpy as jnp
from jax import lax
from jax.experimental import pallas as pl
from jax.experimental.pallas import tpu as pltpu
from jax.sharding import PartitionSpec as P

MESH = pl.DeviceIdType.MESH
F32, BF16 = jnp.float32, jnp.bfloat16
NT = 128
ROUNDS = 7
ROWS = 128
COLS = 256
HALF = 64
CH = 64
HC = 32
PAR = 128
CAP = 192
EMPTY = 2.0**100


def dot(a, b):
    return jnp.dot(a, b, preferred_element_type=F32)


def dot_t(a, b):
    return lax.dot_general(a, b, (((1,), (1,)), ((), ())), preferred_element_type=F32)


def ones_at(shape, test):
    row = lax.broadcasted_iota(jnp.int32, shape, 0)
    col = lax.broadcasted_iota(jnp.int32, shape, 1)
    return jnp.where(test(row, col), 1.0, 0.0).astype(BF16)


def shifted_sum(z, shift, col):
    left = jnp.where(col >= shift, pltpu.roll(z[0:128], shift, 1), 0.0)
    right = jnp.where(col < COLS - shift, pltpu.roll(z[256:384], COLS - shift, 1), 0.0)
    return z[128:256] + left + right


def main_kernel(
    feat, valid, owner, w1raw, w2raw, wmraw,
    enh_out, recv,
    fv, f32t, x, h, e32, et, w1r, w2r, wmr, w1, w2, wm, near, mall, t1, tiles, tall, sel, s32, send,
    fsem, wsem, wsend, wrecv, xsend, xrecv, hsend, hrecv, bsem, esem, tsem, asem,
):
    t = lax.axis_index("tiles")
    c = lax.axis_index("chan")
    sib = 1 - c
    down = lax.rem(t + 1, NT)
    up = lax.rem(t + NT - 1, NT)
    base = HALF * c

    def remote(src, dst, ssem, rsem, tile, core):
        return pltpu.make_async_remote_copy(
            src, dst, ssem, rsem, device_id={"tiles": tile, "chan": core}, device_id_type=MESH
        )

    def partner(r):
        bit = lax.rem(t // 2**r, 2)
        return t + 2**r - bit * 2 ** (r + 1)

    bar = pltpu.get_barrier_semaphore()
    near_by = [(t, sib), (down, 0), (down, 1), (up, 0), (up, 1)]
    for tile, core in near_by + [(partner(r), c) for r in range(ROUNDS)]:
        pl.semaphore_signal(
            bar, inc=1, device_id={"tiles": tile, "chan": core}, device_id_type=MESH
        )

    def chunk_of(i, core):
        return lax.rem(i + 3 * (1 - core), 8)

    def load(i):
        rows = pl.ds(pl.multiple_of(16 * chunk_of(i, c), 16), 16)
        return pltpu.make_async_copy(feat.at[:, rows], fv.at[:, rows], fsem.at[i])

    for i in range(8):
        load(i).start()
    my_ch = pl.ds(pl.multiple_of(c * HC, HC), HC)
    pieces = [(w1raw, w1r.at[:, my_ch]), (w2raw, w2r.at[:, my_ch]), (wmraw, wmr.at[:, my_ch])]
    w_own = [pltpu.make_async_copy(a, b, wsem.at[i]) for i, (a, b) in enumerate(pieces)]
    w_far = [remote(a, b, wsend.at[i], wrecv.at[i], t, sib) for i, (a, b) in enumerate(pieces)]
    w_far.append(remote(valid, near, wsend.at[3], wrecv.at[3], lax.rem(t + 1 - 2 * c + NT, NT), c))
    for copy in w_own:
        copy.start()

    own_row = jnp.broadcast_to(owner[...], (PAR, PAR))
    own_col = jnp.transpose(own_row.astype(F32))
    row_id = lax.broadcasted_iota(jnp.int32, (PAR, PAR), 0)
    col_id = lax.broadcasted_iota(jnp.int32, (PAR, PAR), 1)
    before = jnp.where((own_col == own_row.astype(F32)) & (row_id < col_id), 1.0, 0.0)
    rank = jnp.sum(before, axis=0, keepdims=True)
    for k in range(2):
        hit = (row_id == own_row) & (jnp.broadcast_to(rank, (PAR, PAR)) == float(k))
        sel[pl.ds(k * PAR, PAR)] = jnp.where(hit, 1.0, 0.0).astype(BF16)

    def turn(i):
        load(i).wait()
        k = chunk_of(i, c)
        rows = pl.ds(pl.multiple_of(16 * k, 16), 16)
        for d2 in range(2):
            f32t[d2] = fv[:, rows, pl.ds(d2 * 128, 128)].astype(F32).reshape(512, 128)
        for r in range(16):
            for d2 in range(2):
                x[3 + 16 * k + r, my_ch, pl.ds(d2 * 128, 128)] = f32t[
                    d2, pl.ds(r, HC, stride=16), :
                ].astype(BF16)

    def x_copy(i, core):
        rows = pl.ds(3 + 16 * chunk_of(i, core), 16)
        part = x.at[rows, pl.ds(pl.multiple_of(core * HC, HC), HC)]
        return remote(part, part, xsend.at[i], xrecv.at[i], t, sib)

    turn(0)
    pl.semaphore_wait(bar, 5 + ROUNDS)

    def signal_round(r):
        pl.semaphore_signal(
            bsem.at[r], inc=1, device_id={"tiles": partner(r), "chan": c}, device_id_type=MESH
        )

    signal_round(0)
    for copy in w_far:
        copy.start()
    x_copy(0, c).start()
    for i in range(1, 8):
        turn(i)
        if i < 5:
            x_copy(i, c).start()
    halo = [
        remote(x.at[pl.ds(ROWS, 3), my_ch], x.at[pl.ds(0, 3), my_ch], hsend.at[0], hrecv.at[c], down, 0),
        remote(x.at[pl.ds(3, 3), my_ch], x.at[pl.ds(131, 3), my_ch], hsend.at[1], hrecv.at[c], up, 1),
    ]
    for copy in halo:
        copy.start()

    for copy in w_own:
        copy.wait()
    for copy in w_far:
        copy.wait_recv()
    for raw, out in ((w1r, w1), (w2r, w2)):
        for first in range(2):
            rows = []
            for b in range(3):
                total = jnp.zeros((CH, 256), F32)
                for a in range(3):
                    place = ones_at((CH, 256), lambda i, j, s=a + first: j == i + CH * s)
                    total = total + dot(raw[3 * a + b], place)
                out[2 * b + first] = total.astype(BF16)
    for tr in range(4):
        place = ones_at((CH, 256), lambda i, j, tr=tr: j == (i // HC) * 128 + tr * HC + i % HC)
        for a in range(2):
            for b in range(2):
                wm[b * 8 + tr * 2 + a] = dot(wmr[2 * a + b], place).astype(BF16)
    spread = ones_at((32, COLS), lambda i, j: i == j // 8)
    mine = dot(valid[...].astype(F32).astype(BF16), spread)
    other = dot(near[...].astype(F32).astype(BF16), spread)
    inside_up = jnp.where(t > 0, 1.0, 0.0).astype(F32)
    inside_down = jnp.where(t < NT - 1, 1.0, 0.0).astype(F32)
    mall[0] = jnp.broadcast_to(other[15:16], (8, COLS)) * inside_up
    mall[17] = jnp.broadcast_to(other[0:1], (8, COLS)) * inside_down
    for i in range(16):
        mall[i + 1] = jnp.broadcast_to(mine[i : i + 1], (8, COLS))

    col = lax.broadcasted_iota(jnp.int32, (128, COLS), 1)

    def conv_one(j):
        m = lax.rem(j + 2 * (1 - c), 34)
        z = dot(w1[...].reshape(384, 256), x[pl.ds(base + 2 * m, 4)].reshape(256, COLS))
        out = shifted_sum(z, 1, col).reshape(16, 8, COLS) * mall[8 * c + (m + 3) // 4][None]
        out = jnp.maximum(out, 0.0).reshape(2, CH, COLS).astype(BF16)
        h[0, m] = out[0]
        h[1, m] = out[1]

    def next_round(r):
        pl.semaphore_wait(bsem.at[r], 1)
        if r + 1 < ROUNDS:
            signal_round(r + 1)

    for phase in range(4):
        for i in (0, 1) if phase == 0 else (phase + 1,):
            x_copy(i, sib).wait_recv()
        if phase:
            next_round(phase - 1)

        def four(k, carry, phase=phase):
            for u in range(4):
                conv_one(8 * phase + 4 * k + u)
            return carry

        lax.fori_loop(0, 2, four, 0)

    edge = x.at[pl.ds(131 * c, 3), pl.ds(0, HC)]
    for k in range(2):
        pltpu.make_async_copy(edge, edge, hrecv.at[k]).wait()

    @pl.when((t == 0) & (c == 0))
    def _():
        x[pl.ds(0, 3)] = jnp.zeros((3, CH, COLS), BF16)

    @pl.when((t == NT - 1) & (c == 1))
    def _():
        x[pl.ds(131, 3)] = jnp.zeros((3, CH, COLS), BF16)

    next_round(3)
    conv_one(32)
    conv_one(33)
    next_round(4)

    perm = ones_at((256, 256), lambda i, j: j == 16 * (i % 16) + 2 * (i // 16 % 8) + i // 128)

    def conv_two(q, carry):
        for n2 in range(2):
            n = 2 * q + n2
            rows = [None] * 4
            for p in range(2):
                z = dot(w2[...].reshape(384, 256), h[p, pl.ds(2 * n, 4)].reshape(256, COLS))
                out = shifted_sum(z, 2, col).reshape(2, CH, COLS)
                for i in range(2):
                    r = 4 * n + p + 2 * i
                    row = (out[i] + x[base + r + 3].astype(F32)).reshape(8, 8, COLS)
                    row = (row * mall[1 + 8 * c + q][None]).reshape(CH, COLS)
                    for d2 in range(2):
                        e32[d2, pl.ds(pl.multiple_of(r * CH, CH), CH)] = row[
                            :, d2 * 128 : d2 * 128 + 128
                        ]
                    rows[p + 2 * i] = row.astype(BF16)
            turned = dot_t(perm, jnp.concatenate(rows, axis=0)).astype(BF16)
            t1[q, :, pl.ds(n2 * 256, 256)] = turned[0:128]
            t1[q, :, pl.ds(512 + n2 * 256, 256)] = turned[128:256]
        return carry

    lax.fori_loop(0, 4, conv_two, 0)
    next_round(5)
    lax.fori_loop(4, 8, conv_two, 0)

    for q in range(8):
        g, tp = q // 2, q % 2
        merged = dot(t1[q], wm[...].reshape(1024, 256)).astype(BF16)
        for v in range(8):
            for k in range(2):
                tiles[k, pl.ds(g * 16, 16), pl.ds((v * 2 + tp) * 128, 128)] = merged[
                    v * 16 : v * 16 + 16, k * 128 : k * 128 + 128
                ]

    my_par = pl.ds(pl.multiple_of(base, HALF), HALF)
    t_own = pltpu.make_async_copy(tiles.at[c], tall.at[my_par], wsem.at[0])
    t_far = remote(tiles.at[sib], tall.at[my_par], tsem.at[0], tsem.at[1], t, sib)
    t_far.start()
    t_own.start()
    filled = jnp.sum(sel[...].astype(F32), axis=1, keepdims=True)
    next_round(6)
    t_own.wait()
    t_far.wait()

    for v in range(8):
        out = dot(sel[...], tall[:, pl.ds(v * 256, 256)])
        if v == 0:
            out = jnp.where(jnp.broadcast_to(filled, (256, 256)) > 0.5, out, EMPTY)
        for k in range(2):
            for d2 in range(2):
                s32[d2, pl.ds(v * 2 + k, 128, stride=16), :] = out[
                    k * 128 : k * 128 + 128, d2 * 128 : d2 * 128 + 128
                ]

    def narrow(i, carry):
        for d2 in range(2):
            part = s32[d2, pl.ds(pl.multiple_of(128 * i, 128), 128)]
            send[pl.ds(8 * i, 8), :, pl.ds(d2 * 128, 128)] = part.astype(BF16).reshape(8, 16, 128)
        return carry

    lax.fori_loop(0, 16, narrow, 0)

    def deliver(i, carry):
        d = lax.rem(t + i, NT)
        remote(send.at[d], recv.at[t], asem.at[0], asem.at[1], d, c).start()
        return carry

    lax.fori_loop(1, NT, deliver, 0)
    own = pltpu.make_async_copy(send.at[t], recv.at[t], wsem.at[1])
    own.start()

    def back(k, carry):
        for d2 in range(2):
            et[k, :, pl.ds(d2 * 128, 128)] = e32[d2, pl.ds(k, HALF, stride=CH), :].astype(BF16)
        return carry

    lax.fori_loop(0, CH, back, 0)
    my_rows = pl.ds(pl.multiple_of(base, HALF), HALF)
    e_own = pltpu.make_async_copy(et.at[my_ch], enh_out.at[:, my_rows], wsem.at[2])
    e_far = remote(
        et.at[pl.ds(pl.multiple_of(sib * HC, HC), HC)], enh_out.at[:, my_rows],
        esem.at[0], esem.at[1], t, sib,
    )
    e_far.start()
    e_own.start()
    for copy in w_far + halo:
        copy.wait_send()
    for i in range(5):
        x_copy(i, c).wait_send()
    own.wait()
    e_own.wait()
    e_far.wait()
    others = recv.at[pl.ds(0, NT - 1)]
    gone = send.at[pl.ds(0, NT - 1)]
    pltpu.make_async_copy(gone, gone, asem.at[0]).wait()
    pltpu.make_async_copy(others, others, asem.at[1]).wait()


def main_call(feat, valid, owner, w1raw, w2raw, wmraw):
    any_ = pl.BlockSpec(memory_space=pl.ANY)
    vmem = pl.BlockSpec(memory_space=pltpu.VMEM)
    dma = pltpu.SemaphoreType.DMA
    return pl.pallas_call(
        main_kernel,
        out_shape=(
            jax.ShapeDtypeStruct((HC, ROWS, COLS), BF16),
            jax.ShapeDtypeStruct((NT, 16, 256), BF16),
        ),
        in_specs=[any_, vmem, vmem, any_, any_, any_],
        out_specs=(any_, any_),
        scratch_shapes=[
            pltpu.VMEM((HC, ROWS, COLS), BF16),
            pltpu.VMEM((2, 512, 128), F32),
            pltpu.VMEM((134, CH, COLS), BF16),
            pltpu.VMEM((2, 34, CH, COLS), BF16),
            pltpu.VMEM((2, HALF * CH, 128), F32),
            pltpu.VMEM((CH, HALF, COLS), BF16),
            pltpu.VMEM((9, CH, CH), BF16),
            pltpu.VMEM((9, CH, CH), BF16),
            pltpu.VMEM((4, CH, CH), BF16),
            pltpu.VMEM((6, CH, 256), BF16),
            pltpu.VMEM((6, CH, 256), BF16),
            pltpu.VMEM((16, CH, 256), BF16),
            pltpu.VMEM((16, 32), jnp.int32),
            pltpu.VMEM((18, 8, COLS), F32),
            pltpu.VMEM((8, 128, 1024), BF16),
            pltpu.VMEM((2, HALF, 2048), BF16),
            pltpu.VMEM((PAR, 2048), BF16),
            pltpu.VMEM((256, PAR), BF16),
            pltpu.VMEM((2, 2048, 128), F32),
            pltpu.VMEM((NT, 16, 256), BF16),
            dma((8,)),
            dma((3,)),
            dma((4,)),
            dma((4,)),
            dma((5,)),
            dma((5,)),
            dma((2,)),
            dma((2,)),
            pltpu.SemaphoreType.REGULAR((ROUNDS,)),
            dma((2,)),
            dma((2,)),
            dma((2,)),
        ],
        compiler_params=pltpu.CompilerParams(
            collective_id=0, has_side_effects=True, vmem_limit_bytes=44 << 20
        ),
        name="convs_and_exchange",
    )(feat, valid, owner, w1raw, w2raw, wmraw)


def place_kernel(recv, enh, out, enh_out, r32, o32, sem):
    move = pltpu.make_async_copy(enh, enh_out, sem)
    move.start()

    def widen(i, carry):
        for d2 in range(2):
            part = recv[pl.ds(8 * i, 8), :, pl.ds(d2 * 128, 128)].reshape(128, 128)
            r32[d2, pl.ds(pl.multiple_of(128 * i, 128), 128)] = part.astype(F32)
        return carry

    lax.fori_loop(0, 16, widen, 0)
    here = [jnp.where(r32[0, pl.ds(k, 128, stride=16), :] < EMPTY, 1.0, 0.0) for k in range(2)]
    count = dot_t(ones_at((8, NT), lambda i, j: j == 0), (here[0] + here[1]).astype(BF16))
    start = dot(count.astype(BF16), ones_at((NT, NT), lambda i, j: i < j))
    slot = lax.broadcasted_iota(jnp.int32, (CAP, NT), 0).astype(F32)
    count = jnp.broadcast_to(count[0:1], (CAP, NT))
    start = jnp.broadcast_to(start[0:1], (CAP, NT))
    pick = jnp.concatenate(
        [
            jnp.where((slot == start + float(k)) & (count > float(k)), 1.0, 0.0)
            for k in range(2)
        ],
        axis=1,
    ).astype(BF16)
    same = ones_at((256, 256), lambda i, j: i == j)
    for v in range(8):
        got = jnp.concatenate(
            [
                jnp.concatenate(
                    [r32[d2, pl.ds(v * 2 + k, 128, stride=16), :] for d2 in range(2)], axis=1
                )
                for k in range(2)
            ],
            axis=0,
        ).astype(BF16)
        turned = dot_t(same, dot(pick, got).astype(BF16))
        for u in range(8):
            part = turned[u * HC : u * HC + HC]
            o32[0, pl.ds(u * 8 + v, HC, stride=64), :] = part[:, 0:128]
            o32[1, pl.ds(u * 8 + v, HC, stride=64), pl.ds(0, 64)] = part[:, 128:CAP]

    def narrow(k, carry):
        rows = pl.ds(pl.multiple_of(64 * k, 64), 64)
        out[k, :, pl.ds(0, 128)] = o32[0, rows].astype(BF16)
        out[k, :, pl.ds(128, 64)] = o32[1, rows, pl.ds(0, 64)].astype(BF16)
        return carry

    lax.fori_loop(0, HC, narrow, 0)
    move.wait()


def place_call(recv, enh):
    vmem = pl.BlockSpec(memory_space=pltpu.VMEM)
    any_ = pl.BlockSpec(memory_space=pl.ANY)
    return pl.pallas_call(
        place_kernel,
        out_shape=(
            jax.ShapeDtypeStruct((HC, 64, CAP), BF16),
            jax.ShapeDtypeStruct((HC, ROWS, COLS), BF16),
        ),
        in_specs=[vmem, any_],
        out_specs=(vmem, any_),
        scratch_shapes=[
            pltpu.VMEM((2, 2048, 128), F32),
            pltpu.VMEM((2, 2048, 128), F32),
            pltpu.SemaphoreType.DMA,
        ],
        compiler_params=pltpu.CompilerParams(vmem_limit_bytes=40 << 20),
        name="place_parents",
    )(recv, enh)


def on_device(features, tile_valid, parent_owner, w_first, w_second, w_merge):
    enh, recv = main_call(
        features, tile_valid, parent_owner.reshape(1, PAR), w_first, w_second,
        jnp.transpose(w_merge, (0, 2, 1)),
    )
    parents, enhanced = place_call(recv, enh)
    return (enhanced, jnp.transpose(parents, (0, 2, 1)))


def solution(mesh):
    return jax.shard_map(
        on_device,
        mesh=mesh,
        in_specs=(
            P("chan", "tiles", None),
            P("tiles", None),
            P("tiles"),
            P(None, "chan", None),
            P(None, "chan", None),
            P(None, None, "chan"),
        ),
        out_specs=(P("chan", "tiles", None), P("chan", "tiles", None)),
        check_vma=False,
    )
```

time: 85.5 us -> 71.1 us (0.83); the launches traced: 84.2 us -> 70.8 us
  local copies, waits for them, and re-layouts: 14.5 us -> 5.46 us
  Pallas kernels: 67.7 us -> 64.7 us
  other arithmetic: 1.27 us -> 0 us
    unnamed x11 -> x12, local copies, waits for them, and re-layouts: 9.8 us -> 5.46 us
    pallas_call x2, Pallas kernels: 67.7 us -> 64.7 us  [the longest x1 60 us: main_call(): pl.pallas_call(main_kernel, out_shape=(jax.ShapeDtypeStruct((HC, ROWS, CO...]
    reshape x5 -> x0, local copies, waits for them, and re-layouts: 2.2 us -> none  [the longest x4 2.12 us: toeplitz(): taps = w.reshape(3, 3, HC, CH).transpose(1, 2, 0, 3).reshape(3, HC, 3 * CH)]
    mul x4 -> x0, local copies, waits for them, and re-layouts: 2.05 us -> none  [merge_weights(): w[:, None, :, :, :, None, :] * eye[None, :, None, None, None, :, None]]
    mul x1 -> x0, other arithmetic: 0.97 us -> none  [merge_weights(): w[:, None, :, :, :, None, :] * eye[None, :, None, None, None, :, None]]
where the time goes in v1:
time: 71.1 us; the launch traced here: 70.8 us
  Pallas kernels  64.7 us (91%)
  local copies, waits for them, and re-layouts  5.46 us (8%)
    pallas_call x1, Pallas kernels, main_call(): pl.pallas_call(main_kernel, out_shape=(jax.ShapeDtypeStruct((HC, ROWS, CO...  60 us
    unnamed x12, local copies, waits for them, and re-layouts  5.46 us
    pallas_call x1, Pallas kernels, place_call(): pl.pallas_call(place_kernel, out_shape=(jax.ShapeDtypeStruct((HC, 64, CAP...  4.62 us

profile of v1, /device:TPU:1, one launch (start us, length us, event | category | flops | bytes accessed | tf_op | source)
XLA Modules:
  0.0 70.8 jit_solution(7175374756048031076)
XLA Ops:
  0.6 0.0 copy-start
  0.6 1.6 %copy-done = bf16[32,128,256]{2,1,0:T(8,128)(2,1)S(1)} copy-done((bf16[32,128,256]{2,1,0:T(8,128)(2,1)S(1)}, bf16[32,128,256]{2,1,0:T(8,128)(2,1)}, u32[]{:S(2)}) %copy-start) | copy-done | bytes 2097176
  2.2 0.0 copy-start.1
  2.2 0.9 %copy-done.1 = bf16[9,32,64]{2,1,0:T(8,128)(2,1)S(1)} copy-done((bf16[9,32,64]{2,1,0:T(8,128)(2,1)S(1)}, bf16[9,32,64]{2,1,0:T(8,128)(2,1)}, u32[]{:S(2)}) %copy-start.1) | copy-done | bytes 36888
  3.1 0.0 copy-start.2
  3.1 0.9 %copy-done.2 = bf16[9,32,64]{2,1,0:T(8,128)(2,1)S(1)} copy-done((bf16[9,32,64]{2,1,0:T(8,128)(2,1)S(1)}, bf16[9,32,64]{2,1,0:T(8,128)(2,1)}, u32[]{:S(2)}) %copy-start.2) | copy-done | bytes 36888
  4.0 0.0 copy-start.3
  4.0 0.8 %copy-done.3 = bf16[4,64,32]{1,2,0:T(8,128)(2,1)S(1)} copy-done((bf16[4,64,32]{1,2,0:T(8,128)(2,1)S(1)}, bf16[4,64,32]{1,2,0:T(8,128)(2,1)}, u32[]{:S(2)}) %copy-start.3) | copy-done | bytes 16408
  4.8 0.0 copy-start.4
  4.8 0.7 copy-done.4
  5.4 0.0 copy-start.5
  5.5 0.7 copy-done.5
  6.1 60.0 %convs_and_exchange.1 = (bf16[32,128,256]{2,1,0:T(8,128)(2,1)S(1)}, bf16[128,16,256]{2,1,0:T(8,128)(2,1)S(1)}) custom-call(bf16[32,128,256]{2,1,0:T(8,128)(2,1)S(1)} %copy-done, s32[16,32]{1,0:T(8,128)S(1)} %copy-done.4, s32[1,128]{1,0:T(1,128)S(1)} %bitcast.4, bf16[9,32,64]{2,1,0:T(8,128)(2,1)S(1)} %copy-done.1, bf16[9,32,64]{2,1,0:T(8,128)(2,1)S(1)} %copy-done.2, ...), custom_call_target="tpu_custom_call" | custom-call | tf_op jit(solution)/shard_map/convs_and_exchange/pallas_call | solution.py:317
  66.2 4.6 %place_parents.1 = (bf16[32,64,192]{2,1,0:T(8,128)(2,1)}, bf16[32,128,256]{2,1,0:T(8,128)(2,1)}) custom-call(bf16[128,16,256]{2,1,0:T(8,128)(2,1)S(1)} %get-tuple-element.6.recv, bf16[32,128,256]{2,1,0:T(8,128)(2,1)S(1)} %get-tuple-element.7.enh), custom_call_target="tpu_custom_call" | custom-call | tf_op jit(solution)/shard_map/place_parents/pallas_call | solution.py:420
Async XLA Ops:
  0.6 1.6 %copy-start = (bf16[32,128,256]{2,1,0:T(8,128)(2,1)S(1)}, bf16[32,128,256]{2,1,0:T(8,128)(2,1)}, u32[]{:S(2)}) copy-start(bf16[32,128,256]{2,1,0:T(8,128)(2,1)} %feat.1) | copy-start | bytes 6291460
  2.2 0.9 %copy-start.1 = (bf16[9,32,64]{2,1,0:T(8,128)(2,1)S(1)}, bf16[9,32,64]{2,1,0:T(8,128)(2,1)}, u32[]{:S(2)}) copy-start(bf16[9,32,64]{2,1,0:T(8,128)(2,1)} %w1raw.1) | copy-start | bytes 110596
  3.1 0.9 %copy-start.2 = (bf16[9,32,64]{2,1,0:T(8,128)(2,1)S(1)}, bf16[9,32,64]{2,1,0:T(8,128)(2,1)}, u32[]{:S(2)}) copy-start(bf16[9,32,64]{2,1,0:T(8,128)(2,1)} %w2raw.1) | copy-start | bytes 110596
  4.0 0.8 %copy-start.3 = (bf16[4,64,32]{1,2,0:T(8,128)(2,1)S(1)}, bf16[4,64,32]{1,2,0:T(8,128)(2,1)}, u32[]{:S(2)}) copy-start(bf16[4,64,32]{1,2,0:T(8,128)(2,1)} %param.11) | copy-start | bytes 49156
  4.8 0.7 copy-start.4
  5.4 0.7 copy-start.5

commit v2 on v1

--- a/solution.py
+++ b/solution.py
@@ -10,7 +10,7 @@
 MESH = pl.DeviceIdType.MESH
 F32, BF16 = jnp.float32, jnp.bfloat16
 NT = 128
-ROUNDS = 7
+PLANE, LINE = 16, 8
 ROWS = 128
 COLS = 256
 HALF = 64
@@ -42,10 +42,10 @@
 
 
 def main_kernel(
-    feat, valid, owner, w1raw, w2raw, wmraw,
+    feat, valid_in, owner_in, w1raw, w2raw, wmraw,
     enh_out, recv,
-    fv, f32t, x, h, e32, et, w1r, w2r, wmr, w1, w2, wm, near, mall, t1, tiles, tall, sel, s32, send,
-    fsem, wsem, wsend, wrecv, xsend, xrecv, hsend, hrecv, bsem, esem, tsem, asem,
+    valid, owner, fv, f32t, x, h, e32, et, w1r, w2r, wmr, w1, w2, wm, near, mall, t1, tiles, tall, sel, s32, send,
+    fsem, wsem, wsend, wrecv, xsend, xrecv, hsend, hrecv, bsem, esem, tsend, trecv, asem,
 ):
     t = lax.axis_index("tiles")
     c = lax.axis_index("chan")
@@ -59,13 +59,18 @@
             src, dst, ssem, rsem, device_id={"tiles": tile, "chan": core}, device_id_type=MESH
         )
 
-    def partner(r):
-        bit = lax.rem(t // 2**r, 2)
-        return t + 2**r - bit * 2 ** (r + 1)
+    tx, tz, ty = t // 32, lax.rem(t // 4, LINE), lax.rem(t, 4)
+
+    def in_plane(i):
+        return lax.rem(tx + i // 4, 4) * 32 + tz * 4 + lax.rem(ty + i % 4, 4)
+
+    def in_line(i):
+        return tx * 32 + lax.rem(tz + i, LINE) * 4 + ty
 
     bar = pltpu.get_barrier_semaphore()
     near_by = [(t, sib), (down, 0), (down, 1), (up, 0), (up, 1)]
-    for tile, core in near_by + [(partner(r), c) for r in range(ROUNDS)]:
+    groups = [[in_plane(i) for i in range(1, PLANE)], [in_line(i) for i in range(1, LINE)]]
+    for tile, core in near_by + [(tile, c) for group in groups for tile in group]:
         pl.semaphore_signal(
             bar, inc=1, device_id={"tiles": tile, "chan": core}, device_id_type=MESH
         )
@@ -77,25 +82,21 @@
         rows = pl.ds(pl.multiple_of(16 * chunk_of(i, c), 16), 16)
         return pltpu.make_async_copy(feat.at[:, rows], fv.at[:, rows], fsem.at[i])
 
+    small = [
+        pltpu.make_async_copy(owner_in, owner, wsem.at[3]),
+        pltpu.make_async_copy(valid_in, valid, wsem.at[4]),
+    ]
+    small[0].start()
     for i in range(8):
         load(i).start()
+    small[1].start()
     my_ch = pl.ds(pl.multiple_of(c * HC, HC), HC)
     pieces = [(w1raw, w1r.at[:, my_ch]), (w2raw, w2r.at[:, my_ch]), (wmraw, wmr.at[:, my_ch])]
     w_own = [pltpu.make_async_copy(a, b, wsem.at[i]) for i, (a, b) in enumerate(pieces)]
     w_far = [remote(a, b, wsend.at[i], wrecv.at[i], t, sib) for i, (a, b) in enumerate(pieces)]
-    w_far.append(remote(valid, near, wsend.at[3], wrecv.at[3], lax.rem(t + 1 - 2 * c + NT, NT), c))
+    w_far.append(remote(valid_in, near, wsend.at[3], wrecv.at[3], lax.rem(t + 1 - 2 * c + NT, NT), c))
     for copy in w_own:
         copy.start()
-
-    own_row = jnp.broadcast_to(owner[...], (PAR, PAR))
-    own_col = jnp.transpose(own_row.astype(F32))
-    row_id = lax.broadcasted_iota(jnp.int32, (PAR, PAR), 0)
-    col_id = lax.broadcasted_iota(jnp.int32, (PAR, PAR), 1)
-    before = jnp.where((own_col == own_row.astype(F32)) & (row_id < col_id), 1.0, 0.0)
-    rank = jnp.sum(before, axis=0, keepdims=True)
-    for k in range(2):
-        hit = (row_id == own_row) & (jnp.broadcast_to(rank, (PAR, PAR)) == float(k))
-        sel[pl.ds(k * PAR, PAR)] = jnp.where(hit, 1.0, 0.0).astype(BF16)
 
     def turn(i):
         load(i).wait()
@@ -115,12 +116,13 @@
         return remote(part, part, xsend.at[i], xrecv.at[i], t, sib)
 
     turn(0)
-    pl.semaphore_wait(bar, 5 + ROUNDS)
+    pl.semaphore_wait(bar, 5 + PLANE - 1 + LINE - 1)
 
     def signal_round(r):
-        pl.semaphore_signal(
-            bsem.at[r], inc=1, device_id={"tiles": partner(r), "chan": c}, device_id_type=MESH
-        )
+        for tile in groups[r]:
+            pl.semaphore_signal(
+                bsem.at[r], inc=1, device_id={"tiles": tile, "chan": c}, device_id_type=MESH
+            )
 
     signal_round(0)
     for copy in w_far:
@@ -137,7 +139,18 @@
     for copy in halo:
         copy.start()
 
-    for copy in w_own:
+    small[0].wait()
+    own_row = jnp.broadcast_to(owner[...], (PAR, PAR))
+    own_col = jnp.transpose(own_row.astype(F32))
+    row_id = lax.broadcasted_iota(jnp.int32, (PAR, PAR), 0)
+    col_id = lax.broadcasted_iota(jnp.int32, (PAR, PAR), 1)
+    before = jnp.where((own_col == own_row.astype(F32)) & (row_id < col_id), 1.0, 0.0)
+    rank = jnp.sum(before, axis=0, keepdims=True)
+    for k in range(2):
+        hit = (row_id == own_row) & (jnp.broadcast_to(rank, (PAR, PAR)) == float(k))
+        sel[pl.ds(k * PAR, PAR)] = jnp.where(hit, 1.0, 0.0).astype(BF16)
+
+    for copy in w_own + small[1:]:
         copy.wait()
     for copy in w_far:
         copy.wait_recv()
@@ -175,23 +188,14 @@
         h[0, m] = out[0]
         h[1, m] = out[1]
 
-    def next_round(r):
-        pl.semaphore_wait(bsem.at[r], 1)
-        if r + 1 < ROUNDS:
-            signal_round(r + 1)
-
-    for phase in range(4):
-        for i in (0, 1) if phase == 0 else (phase + 1,):
-            x_copy(i, sib).wait_recv()
-        if phase:
-            next_round(phase - 1)
-
-        def four(k, carry, phase=phase):
-            for u in range(4):
-                conv_one(8 * phase + 4 * k + u)
-            return carry
-
-        lax.fori_loop(0, 2, four, 0)
+    def phase_of_eight(phase, carry):
+        x_copy(phase + 1, sib).wait_recv()
+        for u in range(8):
+            conv_one(8 * phase + u)
+        return carry
+
+    x_copy(0, sib).wait_recv()
+    lax.fori_loop(0, 4, phase_of_eight, 0)
 
     edge = x.at[pl.ds(131 * c, 3), pl.ds(0, HC)]
     for k in range(2):
@@ -205,14 +209,14 @@
     def _():
         x[pl.ds(131, 3)] = jnp.zeros((3, CH, COLS), BF16)
 
-    next_round(3)
     conv_one(32)
     conv_one(33)
-    next_round(4)
+    pl.semaphore_wait(bsem.at[0], PLANE - 1)
+    signal_round(1)
 
     perm = ones_at((256, 256), lambda i, j: j == 16 * (i % 16) + 2 * (i // 16 % 8) + i // 128)
 
-    def conv_two(q, carry):
+    def conv_two(q):
         for n2 in range(2):
             n = 2 * q + n2
             rows = [None] * 4
@@ -231,30 +235,39 @@
             turned = dot_t(perm, jnp.concatenate(rows, axis=0)).astype(BF16)
             t1[q, :, pl.ds(n2 * 256, 256)] = turned[0:128]
             t1[q, :, pl.ds(512 + n2 * 256, 256)] = turned[128:256]
+
+    def pair_of_two(k, carry):
+        conv_two(2 * k)
+        conv_two(2 * k + 1)
         return carry
 
-    lax.fori_loop(0, 4, conv_two, 0)
-    next_round(5)
-    lax.fori_loop(4, 8, conv_two, 0)
-
-    for q in range(8):
-        g, tp = q // 2, q % 2
-        merged = dot(t1[q], wm[...].reshape(1024, 256)).astype(BF16)
-        for v in range(8):
-            for k in range(2):
-                tiles[k, pl.ds(g * 16, 16), pl.ds((v * 2 + tp) * 128, 128)] = merged[
-                    v * 16 : v * 16 + 16, k * 128 : k * 128 + 128
-                ]
-
-    my_par = pl.ds(pl.multiple_of(base, HALF), HALF)
-    t_own = pltpu.make_async_copy(tiles.at[c], tall.at[my_par], wsem.at[0])
-    t_far = remote(tiles.at[sib], tall.at[my_par], tsem.at[0], tsem.at[1], t, sib)
-    t_far.start()
-    t_own.start()
+    my_par = [pl.ds(pl.multiple_of(base + 32 * i, 32), 32) for i in range(2)]
+    half = [pl.ds(32 * i, 32) for i in range(2)]
+    t_own = [
+        pltpu.make_async_copy(tiles.at[c, half[i]], tall.at[my_par[i]], wsem.at[i]) for i in range(2)
+    ]
+    t_far = [
+        remote(tiles.at[sib, half[i]], tall.at[my_par[i]], tsend.at[i], trecv.at[i], t, sib)
+        for i in range(2)
+    ]
+    for part in range(2):
+        lax.fori_loop(2 * part, 2 * part + 2, pair_of_two, 0)
+        four = t1[pl.ds(4 * part, 4)].reshape(512, 1024)
+        merged = dot(four, wm[...].reshape(1024, 256)).astype(BF16)
+        for q4 in range(4):
+            g, tp = 2 * part + q4 // 2, q4 % 2
+            for v in range(8):
+                at = q4 * 128 + v * 16
+                for k in range(2):
+                    tiles[k, pl.ds(g * 16, 16), pl.ds((v * 2 + tp) * 128, 128)] = merged[
+                        at : at + 16, k * 128 : k * 128 + 128
+                    ]
+        t_far[part].start()
+        t_own[part].start()
     filled = jnp.sum(sel[...].astype(F32), axis=1, keepdims=True)
-    next_round(6)
-    t_own.wait()
-    t_far.wait()
+    pl.semaphore_wait(bsem.at[1], LINE - 1)
+    for copy in t_own + t_far:
+        copy.wait()
 
     for v in range(8):
         out = dot(sel[...], tall[:, pl.ds(v * 256, 256)])
@@ -266,20 +279,21 @@
                     k * 128 : k * 128 + 128, d2 * 128 : d2 * 128 + 128
                 ]
 
-    def narrow(i, carry):
+    def deliver(i, carry):
+        eight = lax.rem(t // 8 + i, NT // 8)
         for d2 in range(2):
-            part = s32[d2, pl.ds(pl.multiple_of(128 * i, 128), 128)]
-            send[pl.ds(8 * i, 8), :, pl.ds(d2 * 128, 128)] = part.astype(BF16).reshape(8, 16, 128)
+            part = s32[d2, pl.ds(pl.multiple_of(128 * eight, 128), 128)]
+            send[pl.ds(8 * eight, 8), :, pl.ds(d2 * 128, 128)] = part.astype(BF16).reshape(8, 16, 128)
+        for k in range(8):
+            d = 8 * eight + lax.rem(t + k, 8)
+
+            @pl.when(d != t)
+            def _():
+                remote(send.at[d], recv.at[t], asem.at[0], asem.at[1], d, c).start()
+
         return carry
 
-    lax.fori_loop(0, 16, narrow, 0)
-
-    def deliver(i, carry):
-        d = lax.rem(t + i, NT)
-        remote(send.at[d], recv.at[t], asem.at[0], asem.at[1], d, c).start()
-        return carry
-
-    lax.fori_loop(1, NT, deliver, 0)
+    lax.fori_loop(0, NT // 8, deliver, 0)
     own = pltpu.make_async_copy(send.at[t], recv.at[t], wsem.at[1])
     own.start()
 
@@ -312,7 +326,6 @@
 
 def main_call(feat, valid, owner, w1raw, w2raw, wmraw):
     any_ = pl.BlockSpec(memory_space=pl.ANY)
-    vmem = pl.BlockSpec(memory_space=pltpu.VMEM)
     dma = pltpu.SemaphoreType.DMA
     return pl.pallas_call(
         main_kernel,
@@ -320,9 +333,11 @@
             jax.ShapeDtypeStruct((HC, ROWS, COLS), BF16),
             jax.ShapeDtypeStruct((NT, 16, 256), BF16),
         ),
-        in_specs=[any_, vmem, vmem, any_, any_, any_],
+        in_specs=[pl.BlockSpec(memory_space=pltpu.HBM)] * 6,
         out_specs=(any_, any_),
         scratch_shapes=[
+            pltpu.VMEM((16, 32), jnp.int32),
+            pltpu.VMEM((1, PAR), jnp.int32),
             pltpu.VMEM((HC, ROWS, COLS), BF16),
             pltpu.VMEM((2, 512, 128), F32),
             pltpu.VMEM((134, CH, COLS), BF16),
@@ -344,36 +359,47 @@
             pltpu.VMEM((2, 2048, 128), F32),
             pltpu.VMEM((NT, 16, 256), BF16),
             dma((8,)),
-            dma((3,)),
+            dma((5,)),
             dma((4,)),
             dma((4,)),
             dma((5,)),
             dma((5,)),
             dma((2,)),
             dma((2,)),
-            pltpu.SemaphoreType.REGULAR((ROUNDS,)),
+            pltpu.SemaphoreType.REGULAR((2,)),
+            dma((2,)),
             dma((2,)),
             dma((2,)),
             dma((2,)),
         ],
         compiler_params=pltpu.CompilerParams(
-            collective_id=0, has_side_effects=True, vmem_limit_bytes=44 << 20
+            collective_id=0, has_side_effects=True, vmem_limit_bytes=60 << 20
         ),
         name="convs_and_exchange",
     )(feat, valid, owner, w1raw, w2raw, wmraw)
 
 
-def place_kernel(recv, enh, out, enh_out, r32, o32, sem):
-    move = pltpu.make_async_copy(enh, enh_out, sem)
-    move.start()
-
-    def widen(i, carry):
-        for d2 in range(2):
-            part = recv[pl.ds(8 * i, 8), :, pl.ds(d2 * 128, 128)].reshape(128, 128)
-            r32[d2, pl.ds(pl.multiple_of(128 * i, 128), 128)] = part.astype(F32)
-        return carry
-
-    lax.fori_loop(0, 16, widen, 0)
+def place_kernel(recv, enh, out, enh_out, got16, r32, o, hop, sem, rsem):
+    parts = [pl.ds(8 * i, 8) for i in range(4)]
+    ins = [pltpu.make_async_copy(enh.at[p], hop.at[p], sem.at[i]) for i, p in enumerate(parts)]
+    outs = [pltpu.make_async_copy(hop.at[p], enh_out.at[p], sem.at[i]) for i, p in enumerate(parts)]
+    some = [
+        pltpu.make_async_copy(recv.at[pl.ds(32 * i, 32)], got16.at[pl.ds(32 * i, 32)], rsem.at[i])
+        for i in range(4)
+    ]
+    for copy in some + ins:
+        copy.start()
+
+    for first in range(0, NT, 32):
+        some[first // 32].wait()
+
+        def widen(i, carry):
+            for d2 in range(2):
+                part = got16[pl.ds(8 * i, 8), :, pl.ds(d2 * 128, 128)].reshape(128, 128)
+                r32[d2, pl.ds(pl.multiple_of(128 * i, 128), 128)] = part.astype(F32)
+            return carry
+
+        lax.fori_loop(first // 8, first // 8 + 4, widen, 0)
     here = [jnp.where(r32[0, pl.ds(k, 128, stride=16), :] < EMPTY, 1.0, 0.0) for k in range(2)]
     count = dot_t(ones_at((8, NT), lambda i, j: j == 0), (here[0] + here[1]).astype(BF16))
     start = dot(count.astype(BF16), ones_at((NT, NT), lambda i, j: i < j))
@@ -387,7 +413,7 @@
         ],
         axis=1,
     ).astype(BF16)
-    same = ones_at((256, 256), lambda i, j: i == j)
+    by_four = ones_at((256, 256), lambda i, j: j == i % 32 // 4 * 32 + i // 32 * 4 + i % 4)
     for v in range(8):
         got = jnp.concatenate(
             [
@@ -398,20 +424,28 @@
             ],
             axis=0,
         ).astype(BF16)
-        turned = dot_t(same, dot(pick, got).astype(BF16))
-        for u in range(8):
-            part = turned[u * HC : u * HC + HC]
-            o32[0, pl.ds(u * 8 + v, HC, stride=64), :] = part[:, 0:128]
-            o32[1, pl.ds(u * 8 + v, HC, stride=64), pl.ds(0, 64)] = part[:, 128:CAP]
-
-    def narrow(k, carry):
-        rows = pl.ds(pl.multiple_of(64 * k, 64), 64)
-        out[k, :, pl.ds(0, 128)] = o32[0, rows].astype(BF16)
-        out[k, :, pl.ds(128, 64)] = o32[1, rows, pl.ds(0, 64)].astype(BF16)
-        return carry
-
-    lax.fori_loop(0, HC, narrow, 0)
-    move.wait()
+        o[v] = dot(dot(pick, got).astype(BF16), by_four).astype(BF16)
+    for first, second in zip(ins, outs):
+        first.wait()
+        second.start()
+    turn = ones_at((256, 256), lambda i, j: j == i % 8 * 32 + i // 8 % 8 * 4 + i // 64)
+    lane = lax.broadcasted_iota(jnp.int32, (CAP, 128), 1) // 32
+    for q in range(8):
+        w, pos = q // 4, q % 4
+        halves = []
+        for hv in range(2):
+            acc = jnp.zeros((CAP, 128), BF16)
+            for i in range(4):
+                part = o[hv * 4 + i, :, pl.ds(w * 128, 128)]
+                if i != pos:
+                    part = pltpu.roll(part, (32 * (i - pos)) % 128, 1)
+                acc = jnp.where(lane == i, part, acc)
+            halves.append(acc)
+        last = dot_t(turn, jnp.concatenate(halves, axis=1)).astype(BF16)
+        for i in range(4):
+            out[q * 4 + i] = last[i * 64 : i * 64 + 64]
+    for copy in outs:
+        copy.wait()
 
 
 def place_call(recv, enh):
@@ -423,14 +457,17 @@
             jax.ShapeDtypeStruct((HC, 64, CAP), BF16),
             jax.ShapeDtypeStruct((HC, ROWS, COLS), BF16),
         ),
-        in_specs=[vmem, any_],
+        in_specs=[any_, any_],
         out_specs=(vmem, any_),
         scratch_shapes=[
+            pltpu.VMEM((NT, 16, 256), BF16),
             pltpu.VMEM((2, 2048, 128), F32),
-            pltpu.VMEM((2, 2048, 128), F32),
-            pltpu.SemaphoreType.DMA,
+            pltpu.VMEM((8, CAP, 256), BF16),
+            pltpu.VMEM((HC, ROWS, COLS), BF16),
+            pltpu.SemaphoreType.DMA((4,)),
+            pltpu.SemaphoreType.DMA((4,)),
         ],
-        compiler_params=pltpu.CompilerParams(vmem_limit_bytes=40 << 20),
+        compiler_params=pltpu.CompilerParams(vmem_limit_bytes=60 << 20),
         name="place_parents",
     )(recv, enh)
 

time: 71.1 us -> 62.3 us (0.88)
  local copies, waits for them, and re-layouts: 5.46 us -> 0 us
  Pallas kernels: 64.7 us -> 61.5 us
    unnamed x12 -> x0, local copies, waits for them, and re-layouts: 5.46 us -> none
    pallas_call x1, Pallas kernels: 60 us -> 56 us  [main_call(): pl.pallas_call(main_kernel, out_shape=(jax.ShapeDtypeStruct((HC, ROWS, CO...]
    pallas_call x1, Pallas kernels: 4.62 us -> 5.48 us  [place_call(): pl.pallas_call(place_kernel, out_shape=(jax.ShapeDtypeStruct((HC, 64, CAP...]
where the time goes in v2:
time: 62.3 us; the launch traced here: 62.1 us
  Pallas kernels  61.5 us (99%)
  between operations  0.64 us (1%)
    pallas_call x1, Pallas kernels, main_call(): pl.pallas_call(main_kernel, out_shape=(jax.ShapeDtypeStruct((HC, ROWS, CO...  56 us
    pallas_call x1, Pallas kernels, place_call(): pl.pallas_call(place_kernel, out_shape=(jax.ShapeDtypeStruct((HC, 64, CAP...  5.48 us

profile of v2, /device:TPU:1, one launch (start us, length us, event | category | flops | bytes accessed | tf_op | source)
XLA Modules:
  0.0 62.1 jit_solution(10578456437342873785)
XLA Ops:
  0.6 56.0 %convs_and_exchange.1 = (bf16[32,128,256]{2,1,0:T(8,128)(2,1)}, bf16[128,16,256]{2,1,0:T(8,128)(2,1)}) custom-call(bf16[32,128,256]{2,1,0:T(8,128)(2,1)} %feat.1, s32[16,32]{1,0:T(8,128)} %valid_in.1, s32[1,128]{1,0:T(1,128)} %bitcast.4, bf16[9,32,64]{2,1,0:T(8,128)(2,1)} %w1raw.1, bf16[9,32,64]{2,1,0:T(8,128)(2,1)} %w2raw.1, bf16[4,32,64]{2,1,0:T(8,128)(2,1)} %bitcast.3), custom_call_target="tpu_custom_call" | custom-call | tf_op jit(solution)/shard_map/convs_and_exchange/pallas_call | solution.py:330
  56.7 5.5 %place_parents.1 = (bf16[32,64,192]{2,1,0:T(8,128)(2,1)}, bf16[32,128,256]{2,1,0:T(8,128)(2,1)}) custom-call(bf16[128,16,256]{2,1,0:T(8,128)(2,1)} %get-tuple-element.6.recv, bf16[32,128,256]{2,1,0:T(8,128)(2,1)} %get-tuple-element.7.enh), custom_call_target="tpu_custom_call" | custom-call | tf_op jit(solution)/shard_map/place_parents/pallas_call | solution.py:454

commit v3 on v2

--- a/solution.py
+++ b/solution.py
@@ -115,7 +115,6 @@
         part = x.at[rows, pl.ds(pl.multiple_of(core * HC, HC), HC)]
         return remote(part, part, xsend.at[i], xrecv.at[i], t, sib)
 
-    turn(0)
     pl.semaphore_wait(bar, 5 + PLANE - 1 + LINE - 1)
 
     def signal_round(r):
@@ -124,10 +123,11 @@
                 bsem.at[r], inc=1, device_id={"tiles": tile, "chan": c}, device_id_type=MESH
             )
 
-    signal_round(0)
     for copy in w_far:
         copy.start()
+    turn(0)
     x_copy(0, c).start()
+    signal_round(0)
     for i in range(1, 8):
         turn(i)
         if i < 5:
@@ -138,17 +138,6 @@
     ]
     for copy in halo:
         copy.start()
-
-    small[0].wait()
-    own_row = jnp.broadcast_to(owner[...], (PAR, PAR))
-    own_col = jnp.transpose(own_row.astype(F32))
-    row_id = lax.broadcasted_iota(jnp.int32, (PAR, PAR), 0)
-    col_id = lax.broadcasted_iota(jnp.int32, (PAR, PAR), 1)
-    before = jnp.where((own_col == own_row.astype(F32)) & (row_id < col_id), 1.0, 0.0)
-    rank = jnp.sum(before, axis=0, keepdims=True)
-    for k in range(2):
-        hit = (row_id == own_row) & (jnp.broadcast_to(rank, (PAR, PAR)) == float(k))
-        sel[pl.ds(k * PAR, PAR)] = jnp.where(hit, 1.0, 0.0).astype(BF16)
 
     for copy in w_own + small[1:]:
         copy.wait()
@@ -264,6 +253,17 @@
                     ]
         t_far[part].start()
         t_own[part].start()
+    small[0].wait()
+    own_row = jnp.broadcast_to(owner[...], (PAR, PAR))
+    own_col = jnp.transpose(own_row.astype(F32))
+    row_id = lax.broadcasted_iota(jnp.int32, (PAR, PAR), 0)
+    col_id = lax.broadcasted_iota(jnp.int32, (PAR, PAR), 1)
+    before = jnp.where((own_col == own_row.astype(F32)) & (row_id < col_id), 1.0, 0.0)
+    rank = jnp.sum(before, axis=0, keepdims=True)
+    for k in range(2):
+        hit = (row_id == own_row) & (jnp.broadcast_to(rank, (PAR, PAR)) == float(k))
+        sel[pl.ds(k * PAR, PAR)] = jnp.where(hit, 1.0, 0.0).astype(BF16)
+
     filled = jnp.sum(sel[...].astype(F32), axis=1, keepdims=True)
     pl.semaphore_wait(bsem.at[1], LINE - 1)
     for copy in t_own + t_far:
@@ -379,7 +379,7 @@
     )(feat, valid, owner, w1raw, w2raw, wmraw)
 
 
-def place_kernel(recv, enh, out, enh_out, got16, r32, o, hop, sem, rsem):
+def place_kernel(recv, enh, out, enh_out, got16, r32, o, hop, mine, sem, rsem, psem):
     parts = [pl.ds(8 * i, 8) for i in range(4)]
     ins = [pltpu.make_async_copy(enh.at[p], hop.at[p], sem.at[i]) for i, p in enumerate(parts)]
     outs = [pltpu.make_async_copy(hop.at[p], enh_out.at[p], sem.at[i]) for i, p in enumerate(parts)]
@@ -443,13 +443,16 @@
             halves.append(acc)
         last = dot_t(turn, jnp.concatenate(halves, axis=1)).astype(BF16)
         for i in range(4):
-            out[q * 4 + i] = last[i * 64 : i * 64 + 64]
+            mine[q * 4 + i] = last[i * 64 : i * 64 + 64]
+        outs.append(
+            pltpu.make_async_copy(mine.at[pl.ds(4 * q, 4)], out.at[pl.ds(4 * q, 4)], psem.at[q])
+        )
+        outs[-1].start()
     for copy in outs:
         copy.wait()
 
 
 def place_call(recv, enh):
-    vmem = pl.BlockSpec(memory_space=pltpu.VMEM)
     any_ = pl.BlockSpec(memory_space=pl.ANY)
     return pl.pallas_call(
         place_kernel,
@@ -458,14 +461,16 @@
             jax.ShapeDtypeStruct((HC, ROWS, COLS), BF16),
         ),
         in_specs=[any_, any_],
-        out_specs=(vmem, any_),
+        out_specs=(any_, any_),
         scratch_shapes=[
             pltpu.VMEM((NT, 16, 256), BF16),
             pltpu.VMEM((2, 2048, 128), F32),
             pltpu.VMEM((8, CAP, 256), BF16),
             pltpu.VMEM((HC, ROWS, COLS), BF16),
+            pltpu.VMEM((HC, 64, CAP), BF16),
             pltpu.SemaphoreType.DMA((4,)),
             pltpu.SemaphoreType.DMA((4,)),
+            pltpu.SemaphoreType.DMA((8,)),
         ],
         compiler_params=pltpu.CompilerParams(vmem_limit_bytes=60 << 20),
         name="place_parents",

time: 62.3 us -> 61.7 us (level)
  no operation moved by 1% of the time
where the time goes in v3:
time: 61.7 us; the launch traced here: 61.6 us
  Pallas kernels  60.9 us (99%)
  between operations  0.64 us (1%)
    pallas_call x1, Pallas kernels, main_call(): pl.pallas_call(main_kernel, out_shape=(jax.ShapeDtypeStruct((HC, ROWS, CO...  56 us
    pallas_call x1, Pallas kernels, place_call(): pl.pallas_call(place_kernel, out_shape=(jax.ShapeDtypeStruct((HC, 64, CAP...  4.91 us

profile of v3, /device:TPU:1, one launch (start us, length us, event | category | flops | bytes accessed | tf_op | source)
XLA Modules:
  0.0 61.6 jit_solution(17373572905121800123)
XLA Ops:
  0.6 56.0 %convs_and_exchange.1 = (bf16[32,128,256]{2,1,0:T(8,128)(2,1)}, bf16[128,16,256]{2,1,0:T(8,128)(2,1)}) custom-call(bf16[32,128,256]{2,1,0:T(8,128)(2,1)} %feat.1, s32[16,32]{1,0:T(8,128)} %valid_in.1, s32[1,128]{1,0:T(1,128)} %bitcast.4, bf16[9,32,64]{2,1,0:T(8,128)(2,1)} %w1raw.1, bf16[9,32,64]{2,1,0:T(8,128)(2,1)} %w2raw.1, bf16[4,32,64]{2,1,0:T(8,128)(2,1)} %bitcast.3), custom_call_target="tpu_custom_call" | custom-call | tf_op jit(solution)/shard_map/convs_and_exchange/pallas_call | solution.py:330
  56.7 4.9 %place_parents.1 = (bf16[32,64,192]{2,1,0:T(8,128)(2,1)}, bf16[32,128,256]{2,1,0:T(8,128)(2,1)}) custom-call(bf16[128,16,256]{2,1,0:T(8,128)(2,1)} %get-tuple-element.6.recv, bf16[32,128,256]{2,1,0:T(8,128)(2,1)} %get-tuple-element.7.enh), custom_call_target="tpu_custom_call" | custom-call | tf_op jit(solution)/shard_map/place_parents/pallas_call | solution.py:457

commit v4 on v3

--- a/solution.py
+++ b/solution.py
@@ -230,8 +230,10 @@
         conv_two(2 * k + 1)
         return carry
 
-    my_par = [pl.ds(pl.multiple_of(base + 32 * i, 32), 32) for i in range(2)]
-    half = [pl.ds(32 * i, 32) for i in range(2)]
+    my_par = [
+        pl.ds(pl.multiple_of(base, 16), 48), pl.ds(pl.multiple_of(base + 48, 16), 16)
+    ]
+    half = [pl.ds(0, 48), pl.ds(48, 16)]
     t_own = [
         pltpu.make_async_copy(tiles.at[c, half[i]], tall.at[my_par[i]], wsem.at[i]) for i in range(2)
     ]
@@ -240,11 +242,12 @@
         for i in range(2)
     ]
     for part in range(2):
-        lax.fori_loop(2 * part, 2 * part + 2, pair_of_two, 0)
-        four = t1[pl.ds(4 * part, 4)].reshape(512, 1024)
-        merged = dot(four, wm[...].reshape(1024, 256)).astype(BF16)
-        for q4 in range(4):
-            g, tp = 2 * part + q4 // 2, q4 % 2
+        lax.fori_loop(3 * part, 3 + part, pair_of_two, 0)
+        count = 6 - 4 * part
+        some = t1[pl.ds(6 * part, count)].reshape(128 * count, 1024)
+        merged = dot(some, wm[...].reshape(1024, 256)).astype(BF16)
+        for q4 in range(count):
+            g, tp = 3 * part + q4 // 2, q4 % 2
             for v in range(8):
                 at = q4 * 128 + v * 16
                 for k in range(2):

time: 61.7 us -> 61.8 us (level)
  no operation moved by 1% of the time
where the time goes in v4:
time: 61.8 us; the launch traced here: 61.7 us
  Pallas kernels  61.1 us (99%)
  between operations  0.64 us (1%)
    pallas_call x1, Pallas kernels, main_call(): pl.pallas_call(main_kernel, out_shape=(jax.ShapeDtypeStruct((HC, ROWS, CO...  56.2 us
    pallas_call x1, Pallas kernels, place_call(): pl.pallas_call(place_kernel, out_shape=(jax.ShapeDtypeStruct((HC, 64, CAP...  4.91 us

profile of v4, /device:TPU:1, one launch (start us, length us, event | category | flops | bytes accessed | tf_op | source)
XLA Modules:
  0.0 61.7 jit_solution(18147157463335939214)
XLA Ops:
  0.6 56.2 %convs_and_exchange.1 = (bf16[32,128,256]{2,1,0:T(8,128)(2,1)}, bf16[128,16,256]{2,1,0:T(8,128)(2,1)}) custom-call(bf16[32,128,256]{2,1,0:T(8,128)(2,1)} %feat.1, s32[16,32]{1,0:T(8,128)} %valid_in.1, s32[1,128]{1,0:T(1,128)} %bitcast.4, bf16[9,32,64]{2,1,0:T(8,128)(2,1)} %w1raw.1, bf16[9,32,64]{2,1,0:T(8,128)(2,1)} %w2raw.1, bf16[4,32,64]{2,1,0:T(8,128)(2,1)} %bitcast.3), custom_call_target="tpu_custom_call" | custom-call | tf_op jit(solution)/shard_map/convs_and_exchange/pallas_call | solution.py:333
  56.8 4.9 %place_parents.1 = (bf16[32,64,192]{2,1,0:T(8,128)(2,1)}, bf16[32,128,256]{2,1,0:T(8,128)(2,1)}) custom-call(bf16[128,16,256]{2,1,0:T(8,128)(2,1)} %get-tuple-element.6.recv, bf16[32,128,256]{2,1,0:T(8,128)(2,1)} %get-tuple-element.7.enh), custom_call_target="tpu_custom_call" | custom-call | tf_op jit(solution)/shard_map/place_parents/pallas_call | solution.py:460
